TPU v7x, 32 devices: a whole 2x2x4 slice. The times are simulated.
32 devices in a mesh: grp: 2 (over x), dev: 16 (over z, y, core).
Axes of the slice: x: 2, y: 2, z: 4, core: 2. Of those that a mesh axis runs over, the one named last changes fastest.
Arguments:
- frames: bfloat16 [80, 64, 1408], P('dev'), may hold values from -100 to 100
- trained: int32 [80], replicated, may hold values from 0 to 3071, as said below
- frame_of: int32 [6144], P('dev'), may hold values from 0 to 3071, as said below
- token_cache: bfloat16 [6144, 1408], P('dev'), may hold values from -100 to 100
- norm_gains: float32 [2, 1408], P('grp'), may hold values from 0.1 to 1.9
- proj_weights: bfloat16 [2, 1408, 4224], P('grp'), may hold values from -4 to 4
- out_weights: bfloat16 [2, 1408, 1408], P('grp'), may hold values from -0.15625 to 0.15625
- patch_cotangent: bfloat16 [80, 64, 1408], P('dev'), may hold values from -0.119628906 to 0.119628906
- time_cotangent: bfloat16 [6144, 1408], P('dev'), may hold values from -6 to 6
Outputs:
- weight_grad: float32 [2, 1408, 1408], P('grp', 'dev')
Inputs may be any that keep to these rules, and one draw needn't show every extreme that they name: `trained`: 80 different frames of the video; among them, for every k, the frames k * 192 and (k + 1) * 192 - 1. `frame_of`: never falls along the tokens; tokens 4 m to 4 m + 3 belong to frames 2 m and 2 m + 1, each frame having 1 to 3 tokens.
All inputs are finite; a program needn't handle non-finite values.
Results may differ from a plain program's by a relative error of at most 0.0078.
Values may be sent and summed in bfloat16 or wider, within the bound.
A program may use at most 192 MiB of HBM per device.

v0:
```python
import jax
import jax.numpy as jnp
from jax import lax
from jax.sharding import PartitionSpec as P

HEADS = 16
HEAD_DIM = 88
SPAN = 128
EPS = 1e-06
HIGH_PRECISION = lax.Precision.HIGHEST


def from_behind(value, axis, steps):
    count = lax.axis_size(axis)
    initial, last = (max(0, -steps), min(count, count - steps))
    return lax.ppermute(value, axis, [(source, source + steps) for source in range(initial, last)])


def with_halo(array, sides, width):
    for axis, dim in sides:
        size, length = (lax.axis_size(axis), array.shape[dim])
        up = [(i, (i + 1) % size) for i in range(size - 1)]
        down = [(j, i) for i, j in up]
        last = lax.slice_in_dim(array, length - width, length, axis=dim)
        initial = lax.slice_in_dim(array, 0, width, axis=dim)
        before = lax.ppermute(last, axis, up)
        after = lax.ppermute(initial, axis, down)
        array = jnp.concatenate([before, array, after], axis=dim)
    return array


def normalize(rows):
    inverse = lax.rsqrt(jnp.mean(rows * rows, axis=-1, keepdims=True) + EPS)
    return (rows * inverse, inverse)


def when_true(flag, compute):

    def skipped():
        return jax.tree.map(jnp.zeros_like, compute())

    return lax.cond(flag, compute, skipped)


def contract_rows(left, right):
    return lax.dot_general(
        left, right, (((0,), (0,)), ((), ())), preferred_element_type=jnp.float32
    )


def contract_exact(left, right):
    return lax.dot_general(left, right, (((0,), (0,)), ((), ())), precision=HIGH_PRECISION)


def contract_cols(left, right):
    return lax.dot_general(
        left, right, (((1,), (1,)), ((), ())), preferred_element_type=jnp.float32
    )


def stack_windows(extended, count):
    return jnp.stack([extended[block * SPAN : (block + 3) * SPAN] for block in range(count)])


def shards(
    frames,
    trained,
    frame_of,
    token_cache,
    norm_gains,
    proj_weights,
    out_weights,
    patch_cotangent,
    time_cotangent,
):
    spatial = lax.axis_index("grp") == 0
    temporal = jnp.logical_not(spatial)
    norm_gain = norm_gains[0]
    in_proj = proj_weights[0]
    out_proj = out_weights[0]
    width = in_proj.shape[0]
    frame_count, patches, _ = frames.shape
    token_count = token_cache.shape[0]
    nblocks = token_count // SPAN
    score_scale = HEAD_DIM ** (-0.5)
    first_token = lax.axis_index("dev") * token_count
    token_total = lax.axis_size("dev") * token_count
    win_pos = (
        first_token
        + (jnp.arange(nblocks, dtype=jnp.int32)[:, None] - 1) * SPAN
        + jnp.arange(3 * SPAN, dtype=jnp.int32)[None, :]
    )
    win_valid = (win_pos >= 0) & (win_pos < token_total)

    def spatial_forward():
        rows = frames.reshape(frame_count * patches, width).astype(jnp.float32)
        scaled_rows, _ = normalize(rows)
        normed = (scaled_rows * norm_gain).astype(jnp.bfloat16)
        packed = jnp.dot(normed, in_proj, preferred_element_type=jnp.float32).astype(jnp.bfloat16)
        packed = packed.reshape(frame_count, patches, 3, HEADS, HEAD_DIM)
        attention_logits = (
            jnp.einsum(
                "fphd,fqhd->fhpq",
                packed[:, :, 0],
                packed[:, :, 1],
                preferred_element_type=jnp.float32,
            )
            * score_scale
        )
        attention_probs = jax.nn.softmax(attention_logits, axis=-1).astype(jnp.bfloat16)
        attended_output = jnp.einsum(
            "fhpq,fqhd->fphd", attention_probs, packed[:, :, 2], preferred_element_type=jnp.float32
        )
        attended_output = attended_output.astype(jnp.bfloat16).reshape(frame_count * patches, width)
        output = rows + jnp.dot(attended_output, out_proj, preferred_element_type=jnp.float32)
        pooled = jnp.mean(output.reshape(frame_count, patches, width), axis=1).astype(jnp.bfloat16)
        return (pooled, attended_output)

    pooled, spatial_mixed = when_true(spatial, spatial_forward)
    handed = from_behind(pooled, "grp", 1)
    arrived = lax.all_gather(handed, "dev", axis=0, tiled=True)

    def temporal_front():
        selector = (frame_of[:, None] == trained[None, :]).astype(jnp.bfloat16)
        inputs = token_cache.astype(jnp.float32) + jnp.dot(
            selector, arrived, preferred_element_type=jnp.float32
        )
        scaled_rows, inverse = normalize(inputs)
        normed = (scaled_rows * norm_gain).astype(jnp.bfloat16)
        packed = jnp.dot(normed, in_proj, preferred_element_type=jnp.float32).astype(jnp.bfloat16)
        return (selector, scaled_rows, inverse, packed[:, :width], packed[:, width:])

    selector, scaled_rows, inverse, queries, key_value = when_true(temporal, temporal_front)
    extended = with_halo(key_value, (("dev", 0),), SPAN)
    key_window = stack_windows(extended, nblocks)
    key_heads = key_window[..., :width].reshape(nblocks, 3 * SPAN, HEADS, HEAD_DIM)
    value_heads = key_window[..., width:].reshape(nblocks, 3 * SPAN, HEADS, HEAD_DIM)
    query_heads = queries.reshape(nblocks, SPAN, HEADS, HEAD_DIM)

    def temporal_attend():
        attention_logits = (
            jnp.einsum(
                "bqhd,bkhd->bhqk", query_heads, key_heads, preferred_element_type=jnp.float32
            )
            * score_scale
        )
        attention_logits = jnp.where(win_valid[:, None, None, :], attention_logits, -1e30)
        row_top = jnp.max(attention_logits, axis=-1, keepdims=True)
        log_total = row_top + jnp.log(
            jnp.sum(jnp.exp(attention_logits - row_top), axis=-1, keepdims=True)
        )
        chances = jnp.exp(attention_logits - log_total)
        chance_weights = chances.astype(jnp.bfloat16)
        attended_output = jnp.einsum(
            "bhqk,bkhd->bqhd", chance_weights, value_heads, preferred_element_type=jnp.float32
        )
        return (
            chances,
            chance_weights,
            log_total[..., 0],
            attended_output.astype(jnp.bfloat16).reshape(token_count, width),
        )

    chances, chance_weights, log_total, time_mixed = when_true(temporal, temporal_attend)

    def temporal_grads():
        grad_mixed = contract_cols(time_cotangent, out_proj).astype(jnp.bfloat16)
        grad_heads = grad_mixed.reshape(nblocks, SPAN, HEADS, HEAD_DIM)
        mixed_heads = time_mixed.reshape(nblocks, SPAN, HEADS, HEAD_DIM)
        row_delta = jnp.sum(
            grad_heads.astype(jnp.float32) * mixed_heads.astype(jnp.float32), axis=-1
        ).transpose(0, 2, 1)
        probability_gradient = jnp.einsum(
            "bqhd,bkhd->bhqk", grad_heads, value_heads, preferred_element_type=jnp.float32
        )
        logit_gradient = (chances * (probability_gradient - row_delta[..., None])).astype(
            jnp.bfloat16
        )
        query_gradient = (
            jnp.einsum(
                "bhqk,bkhd->bqhd", logit_gradient, key_heads, preferred_element_type=jnp.float32
            )
            * score_scale
        )
        return (grad_mixed, row_delta, logit_gradient, query_gradient.reshape(token_count, width))

    grad_mixed, row_delta, logit_gradient, query_gradient = when_true(temporal, temporal_grads)
    stats = jnp.concatenate(
        [
            log_total.transpose(0, 2, 1).reshape(token_count, HEADS),
            row_delta.transpose(0, 2, 1).reshape(token_count, HEADS),
        ],
        axis=-1,
    )
    near_stats = with_halo(stats, (("dev", 0),), SPAN)
    near_rows = with_halo(jnp.concatenate([queries, grad_mixed], axis=-1), (("dev", 0),), SPAN)

    def rim_keys():
        row_window = stack_windows(near_rows, nblocks)
        stat_window = stack_windows(near_stats, nblocks)
        query_part = row_window[..., :width].reshape(nblocks, 3 * SPAN, HEADS, HEAD_DIM)
        grad_part = row_window[..., width:].reshape(nblocks, 3 * SPAN, HEADS, HEAD_DIM)
        totals = stat_window[..., :HEADS].transpose(0, 2, 1)
        deltas = stat_window[..., HEADS:].transpose(0, 2, 1)
        own_keys = key_value[:, :width].reshape(nblocks, SPAN, HEADS, HEAD_DIM)
        own_values = key_value[:, width:].reshape(nblocks, SPAN, HEADS, HEAD_DIM)
        attention_logits = (
            jnp.einsum("bqhd,bkhd->bhqk", query_part, own_keys, preferred_element_type=jnp.float32)
            * score_scale
        )
        again = jnp.where(
            win_valid[:, None, :, None],
            jnp.exp(
                jnp.where(win_valid[:, None, :, None], attention_logits - totals[..., None], 0.0)
            ),
            0.0,
        )
        probability_gradient = jnp.einsum(
            "bqhd,bkhd->bhqk", grad_part, own_values, preferred_element_type=jnp.float32
        )
        part_score = (again * (probability_gradient - deltas[..., None])).astype(jnp.bfloat16)
        key_gradient = (
            jnp.einsum(
                "bhqk,bqhd->bkhd", part_score, query_part, preferred_element_type=jnp.float32
            )
            * score_scale
        )
        value_gradient = jnp.einsum(
            "bhqk,bqhd->bkhd",
            again.astype(jnp.bfloat16),
            grad_part,
            preferred_element_type=jnp.float32,
        )
        return jnp.concatenate(
            [key_gradient.reshape(token_count, width), value_gradient.reshape(token_count, width)],
            axis=-1,
        )

    key_grads = when_true(temporal, rim_keys)

    def temporal_back():
        grad_packed = jnp.concatenate([query_gradient, key_grads], axis=-1).astype(jnp.bfloat16)
        grad_scaled = contract_cols(grad_packed, in_proj) * norm_gain
        grad_inputs = inverse * (
            grad_scaled - scaled_rows * jnp.mean(grad_scaled * scaled_rows, axis=-1, keepdims=True)
        ) + time_cotangent.astype(jnp.float32)
        return contract_exact(selector.astype(jnp.float32), grad_inputs)

    frame_grads = when_true(temporal, temporal_back)
    reduced = lax.psum_scatter(frame_grads, "dev", scatter_dimension=0, tiled=True)
    returned = from_behind(reduced, "grp", -1)

    def spatial_right():
        grads = patch_cotangent.astype(jnp.float32) + returned[:, None, :] / patches
        return grads.reshape(frame_count * patches, width)

    right_side = when_true(spatial, spatial_right)

    def from_frames():
        return contract_exact(spatial_mixed.astype(jnp.float32), right_side)

    def from_tokens():
        return contract_rows(time_mixed, time_cotangent)

    weight_part = lax.psum_scatter(
        lax.cond(spatial, from_frames, from_tokens), "dev", scatter_dimension=0, tiled=True
    )
    return weight_part[None]


def solution(mesh):
    in_specs = (
        P("dev", None, None),
        P(),
        P("dev"),
        P("dev", None),
        P("grp", None),
        P("grp", None, None),
        P("grp", None, None),
        P("dev", None, None),
        P("dev", None),
    )
    out_specs = P("grp", "dev", None)
    return jax.shard_map(shards, mesh=mesh, in_specs=in_specs, out_specs=out_specs, check_vma=False)
```

profile of v0, /device:TPU:0, one launch (start us, length us, event | category | flops | bytes accessed | tf_op | source)
XLA Modules:
  0.0 491.3 jit_solution(10621586428022382250)
XLA Ops:
  6.5 40.0 %conditional.8 = (bf16[5,1408]{1,0:T(8,128)(2,1)S(1)}, bf16[320,1408]{1,0:T(8,128)(2,1)}) conditional(s32[]{:T(128)} %convert_element_type.90, () %tuple.65, (bf16[5,64,1408]{2,1,0:T(8,128)(2,1)}, f32[1,1408]{1,0:T(1,128)}, bf16[1408,4224]{1,0:T(8,128)(2,1)}, bf16[1408,1408]{1,0:T(8,128)(2,1)}) %tuple.143), branch_computations={%region_0.0_spmd, %region_1.0_spmd} | conditional | flops 5198732288 | bytes 54580020 | solution.py:42
  10.3 9.1 %convolution_convert_fusion.1 = bf16[320,4224]{1,0:T(8,128)(2,1)S(1)} fusion(bf16[320,1408]{1,0:T(8,128)(2,1)S(1)} %fusion.44, bf16[1408,4224]{1,0:T(8,128)(2,1)} %get-tuple-element.100), kind=kOutput, calls=%fused_computation.55 | convolution fusion | flops 3807682560 | bytes 15499264 | tf_op jit(solution)/shard_map/cond/branch_1_fun/dot_general | solution.py:99
  19.4 8.5 %reshape.116 = bf16[5,64,3,16,88]{4,3,2,1,0:T(8,128)(2,1)} reshape(bf16[320,4224]{1,0:T(8,128)(2,1)S(1)} %convolution_convert_fusion.1) | data formatting | bytes 5406720 | tf_op jit(solution)/shard_map/cond/branch_1_fun/reshape | solution.py:100
  27.9 3.0 fusion.76
  31.8 3.9 fusion.77
  39.6 5.3 %convolution_add_fusion = f32[320,1408]{1,0:T(8,128)} fusion(bf16[320,1408]{1,0:T(8,128)(2,1)} %reshape.117, bf16[1408,1408]{1,0:T(8,128)(2,1)} %get-tuple-element.101, bf16[320,1408]{1,0:T(8,128)(2,1)S(1)} %bitcast.144), kind=kOutput, calls=%fused_computation.56 | convolution fusion | flops 1269678080 | bytes 7569408 | tf_op jit(solution)/shard_map/cond/branch_1_fun/dot_general | solution.py:115
  49.3 24.1 %all-gather = bf16[16,5,1408]{2,1,0:T(8,128)(2,1)S(1)} all-gather(bf16[1,5,1408]{2,1,0:T(8,128)(2,1)S(1)} %bitcast.152), channel_id=1, replica_groups=mesh['grp'=2,'dev'=16] {'dev'}, dimensions={0}, use_global_device_ids=true | all-gather | bytes 239360 | tf_op jit(solution)/shard_map/all_gather | solution.py:121
  73.5 4.5 conditional.9
  79.4 2.9 copy.69
  83.3 3.1 collective-permute-start.1
  87.7 2.3 constant_dynamic-update-slice_fusion.1
  96.0 6.1 %conditional.10 = (f32[3,16,128,384]{3,2,1,0:T(8,128)}, f32[3,16,128]{2,1,0:T(8,128)S(1)}, bf16[384,1408]{0,1:T(8,128)(2,1)}) conditional(s32[]{:T(128)} %convert_element_type.91, () %tuple.63, (pred[3,384]{1,0:T(4,128)(4,1)S(1)}, bf16[3,128,16,88]{1,0,3,2:T(4,128)(2,1)}, bf16[3,384,16,88]{1,3,2,0:T(8,128)(2,1)S(1)}, ...), branch_computations={%region_9.0_spmd, %region_10.13_spmd} | conditional | flops 856958976 | bytes 60534224 | solution.py:42
  96.0 4.8 broadcast.154
  102.1 6.0 %conditional.11 = (f32[3,16,128]{2,0,1:T(4,128)S(1)}, bf16[384,1408]{0,1:T(8,128)(2,1)}, bf16[384,1408]{0,1:T(8,128)(2,1)}) conditional(s32[]{:T(128)} %convert_element_type.91, () %tuple.72, (bf16[384,1408]{1,0:T(8,128)(2,1)}, bf16[1408,1408]{1,0:T(8,128)(2,1)}, bf16[384,1408]{0,1:T(8,128)(2,1)}, bf16[3,384,16,88]{1,3,2,0:T(8,128)(2,1)}, ...), branch_computations={%region_13.14_spmd, %region_14.16_spmd} | conditional | flops 2363320320 | bytes 39649360 | solution.py:42
  108.0 2.3 constant_dynamic-update-slice_fusion
  111.9 13.2 %collective-permute-start.3 = (bf16[128,2816]{0,1:T(8,128)(2,1)S(1)}, bf16[128,2816]{0,1:T(8,128)(2,1)S(1)}, u32[]{:S(2)}, u32[]{:S(2)}) collective-permute-start(bf16[128,2816]{0,1:T(8,128)(2,1)S(1)} %get-tuple-element.261), channel_id=1, source_target_pairs={{0,1},{1,2},{2,3},{3,4},{4,5},{5,6},{6,7},{7,8},{8,9},{9,10},{10,1... | collective-permute-start | bytes 2162696 | tf_op jit(solution)/shard_map/ppermute | solution.py:26
  126.5 5.0 %collective-permute-start.5 = (f32[128,32]{0,1:T(8,128)S(1)}, f32[128,32]{0,1:T(8,128)S(1)}, u32[]{:S(2)}, u32[]{:S(2)}) collective-permute-start(f32[128,32]{0,1:T(8,128)S(1)} %get-tuple-element.267), channel_id=1, source_target_pairs={{0,1},{1,2},{2,3},{3,4},{4,5},{5,6},{6,7},{7,8},{8,9},{9,10},{10,1... | collective-permute-start | bytes 49160 | tf_op jit(solution)/shard_map/ppermute | solution.py:26
  132.7 3.0 collective-permute-done.6
  139.0 8.4 %conditional.13 = (f32[80,1408]{1,0:T(8,128)}) conditional(s32[]{:T(128)} %convert_element_type.91, () %tuple.71, (f32[384,1]{0,1:T(1,128)S(1)}, bf16[384,1408]{0,1:T(8,128)(2,1)}, bf16[384,2816]{0,1:T(8,128)(2,1)S(1)}, bf16[1408,4224]{1,0:T(8,128)(2,1)}, f32[1,1408]{1,0:T(1,128)}, /*index=5*/f32[384,1408]{1,0:T(8,128)}, ...), branch_computations={%region_18.19_spmd, %region_19.21_spmd} | conditional | flops 5097455616 | bytes 36246600 | solution.py:42
  148.7 213.6 %all-reduce.4.cloned.1.call-done = f32[80,1408]{1,0:T(8,128)} async-done(((f32[80,1408]{1,0:T(8,128)}), f32[80,1408]{1,0:T(8,128)}) %all-reduce.4.cloned.1.call-update) | async-done | bytes 450576
  364.5 4.7 collective-permute-done.7
  370.6 10.3 %conditional.15 = (f32[1408,1408]{1,0:T(8,128)}) conditional(s32[]{:T(128)} %convert_element_type.90, (bf16[384,1408]{0,1:T(8,128)(2,1)}, bf16[384,1408]{1,0:T(8,128)(2,1)S(1)}) %tuple.137, (bf16[320,1408]{1,0:T(8,128)(2,1)}, f32[320,1408]{1,0:T(8,128)S(1)}) %tuple.78), branch_computations={%region_24.25_spmd, %region_25.26_spmd} | conditional | flops 7612661760 | bytes 10633224 | solution.py:266
  370.6 10.3 %fusion.83 = f32[1408,1408]{1,0:T(8,128)} fusion(bf16[320,1408]{1,0:T(8,128)(2,1)} %get-tuple-element.136, f32[320,1408]{1,0:T(8,128)S(1)} %get-tuple-element.137), kind=kOutput, calls=%fused_computation.129 | convolution fusion | flops 7612661760 | bytes 10633216 | tf_op jit(solution)/shard_map/cond/branch_1_fun/dot_general | solution.py:52
  381.0 103.3 %reduce-scatter.4.cloned.1.call-done = f32[88,1408]{1,0:T(8,128)} async-done(((f32[1408,1408]{1,0:T(8,128)}), f32[88,1408]{1,0:T(8,128)}) %reduce-scatter.4.cloned.1.call-update) | async-done | bytes 495632
  (76 shorter events, 44.1 us)
Async XLA Ops:
  6.5 355.7 %all-reduce.4.cloned.1.call-start = ((), (), s32[]{:S(2)}) async-start(), calls=%async_computation.1 | async-start | bytes 901120
  6.5 67.0 %copy-start.15 = (s32[384]{0:T(512)S(1)}, s32[384]{0:T(512)}, u32[]{:S(2)}) copy-start(s32[384]{0:T(512)} %param.27) | copy-start | bytes 4612
  6.5 67.0 %copy-start.16 = (s32[80]{0:T(128)S(1)}, s32[80]{0:T(128)}, u32[]{:S(2)}) copy-start(s32[80]{0:T(128)} %param.26) | copy-start | bytes 964
  36.5 3.1 copy-start.7
  46.5 2.8 collective-permute-start
  78.0 1.3 copy-start.2
  83.3 6.8 %collective-permute-start.1 = (bf16[128,2816]{0,1:T(8,128)(2,1)}, bf16[128,2816]{0,1:T(8,128)(2,1)}, u32[]{:S(2)}, u32[]{:S(2)}) collective-permute-start(bf16[128,2816]{0,1:T(8,128)(2,1)} %get-tuple-element.265), channel_id=1, source_target_pairs={{0,1},{1,2},{2,3},{3,4},{4,5},{5,6},{6,7},{7,8},{8,9},{9,10},{10,1... | collective-permute-start | bytes 2162696 | tf_op jit(solution)/shard_map/ppermute | solution.py:26
  86.4 4.2 collective-permute-start.2
  94.3 1.7 copy-start
  110.4 25.4 %copy-start.1 = (bf16[384,2816]{0,1:T(8,128)(2,1)S(1)}, bf16[384,2816]{0,1:T(8,128)(2,1)}, u32[]{:S(2)}) copy-start(bf16[384,2816]{0,1:T(8,128)(2,1)} %constant_dynamic-update-slice_fusion) | copy-start | bytes 6488068
  111.9 23.8 %collective-permute-start.3 = (bf16[128,2816]{0,1:T(8,128)(2,1)S(1)}, bf16[128,2816]{0,1:T(8,128)(2,1)S(1)}, u32[]{:S(2)}, u32[]{:S(2)}) collective-permute-start(bf16[128,2816]{0,1:T(8,128)(2,1)S(1)} %get-tuple-element.261), channel_id=1, source_target_pairs={{0,1},{1,2},{2,3},{3,4},{4,5},{5,6},{6,7},{7,8},{8,9},{9,10},{10,1... | collective-permute-start | bytes 2162696 | tf_op jit(solution)/shard_map/ppermute | solution.py:26
  125.1 10.7 %collective-permute-start.4 = (bf16[128,2816]{0,1:T(8,128)(2,1)S(1)}, bf16[128,2816]{0,1:T(8,128)(2,1)S(1)}, u32[]{:S(2)}, u32[]{:S(2)}) collective-permute-start(bf16[128,2816]{0,1:T(8,128)(2,1)S(1)} %get-tuple-element.262), channel_id=1, source_target_pairs={{1,0},{2,1},{3,2},{4,3},{5,4},{6,5},{7,6},{8,7},{9,8},{10,9},{11,1... | collective-permute-start | bytes 2162696 | tf_op jit(solution)/shard_map/ppermute | solution.py:27
  126.5 6.3 %collective-permute-start.5 = (f32[128,32]{0,1:T(8,128)S(1)}, f32[128,32]{0,1:T(8,128)S(1)}, u32[]{:S(2)}, u32[]{:S(2)}) collective-permute-start(f32[128,32]{0,1:T(8,128)S(1)} %get-tuple-element.267), channel_id=1, source_target_pairs={{0,1},{1,2},{2,3},{3,4},{4,5},{5,6},{6,7},{7,8},{8,9},{9,10},{10,1... | collective-permute-start | bytes 49160 | tf_op jit(solution)/shard_map/ppermute | solution.py:26
  131.4 4.3 collective-permute-start.6
  135.8 2.6 copy-start.3
  139.0 8.5 %copy-start.17 = (u32[32]{0:T(128)S(1)}, u32[32]{0:T(128)}, u32[]{:S(2)}) copy-start(u32[32]{0:T(128)} %constant.101) | copy-start | bytes 388
  147.5 336.8 %reduce-scatter.4.cloned.1.call-start = ((), (), s32[]{:S(2)}) async-start(), calls=%async_computation.2 | async-start | bytes 8425472
  363.2 6.0 %collective-permute-start.7 = (f32[5,1408]{1,0:T(8,128)S(1)}, f32[5,1408]{1,0:T(8,128)S(1)}, u32[]{:S(2)}, u32[]{:S(2)}) collective-permute-start(f32[5,1408]{1,0:T(8,128)S(1)} %constant_dynamic-slice_fusion), channel_id=1, source_target_pairs={{16,0},{17,1},{18,2},{19,3},{20,4},{21,5},{22,6},{23,7},{24,8},{25... | collective-permute-start | bytes 84488 | tf_op jit(solution)/shard_map/ppermute | solution.py:16
  369.1 1.5 copy-start.5
Sparse Core Ops, SparseCore 0:
  147.6 214.6 all-reduce.3
  381.1 103.1 reduce-scatter.3
where the time goes:
time: 500 us; the launch traced here: 491 us
  waiting for transfers between devices  327 us (65%)
  local copies, waits for them, and re-layouts  44.1 us (9%)
  starting transfers between devices  27.7 us (6%)
  matrix products  26.3 us (5%)
  blocking collectives  24.1 us (5%)
  other arithmetic  15.8 us (3%)
  between operations  14.4 us (3%)
  loops' own time  12.3 us (2%)
    unnamed x4, waiting for transfers between devices  317 us
    all_gather x1, blocking collectives, shards(): arrived = lax.all_gather(handed, 'dev', axis=0, tiled=True)  24.1 us
    ppermute x3, starting transfers between devices, with_halo(): before = lax.ppermute(last, axis, up)  21.2 us
    another operation x7, loops' own time, when_true(): return lax.cond(flag, compute, skipped)  12.3 us
    another operation x13, local copies, waits for them, and re-layouts  11.9 us
    dot_general x1, matrix products, contract_exact(): lax.dot_general(left, right, (((0,), (0,)), ((), ())), precision=HIGH_PRE...  10.3 us
  transfers between devices with their start and end apart: 10, of which 6 were waited for; matrix products, arithmetic and copies ran while one was open for 1% of the time, Pallas kernels for 0%

commit v1 on v0

--- a/solution.py
+++ b/solution.py
@@ -118,7 +118,21 @@
 
     pooled, spatial_mixed = when_true(spatial, spatial_forward)
     handed = from_behind(pooled, "grp", 1)
-    arrived = lax.all_gather(handed, "dev", axis=0, tiled=True)
+    ways, here, step = (lax.axis_size("dev"), lax.axis_index("dev"), handed.shape[0])
+    lengths = [n * ways if d == 0 else n for d, n in enumerate(handed.shape)]
+    full = lax.dynamic_update_slice_in_dim(
+        jnp.zeros(lengths, handed.dtype), handed, here * step, axis=0
+    )
+    going_up = going_down = handed
+    for far in range(1, ways // 2 + 1):
+        going_up = lax.ppermute(going_up, "dev", [(d, (d + 1) % ways) for d in range(ways)])
+        full = lax.dynamic_update_slice_in_dim(full, going_up, (here - far) % ways * step, axis=0)
+        if 2 * far < ways:
+            going_down = lax.ppermute(going_down, "dev", [(d, (d - 1) % ways) for d in range(ways)])
+            full = lax.dynamic_update_slice_in_dim(
+                full, going_down, (here + far) % ways * step, axis=0
+            )
+    arrived = full
 
     def temporal_front():
         selector = (frame_of[:, None] == trained[None, :]).astype(jnp.bfloat16)

time: 500 us -> 519 us (1.038)
  blocking collectives: 24.1 us -> 0 us
  starting transfers between devices: 27.7 us -> 51.5 us
  waiting for transfers between devices: 327 us -> 345 us
    ppermute x0 -> x15, starting transfers between devices: none -> 31.5 us  [the longest x7 31.4 us: shards(): lax.ppermute(going_down, 'dev', [(d, (d - 1) % ways) for d in range(ways)])]
    all_gather x1 -> x0, blocking collectives: 24.1 us -> none  [shards(): arrived = lax.all_gather(handed, 'dev', axis=0, tiled=True)]
    ppermute x0 -> x15, waiting for transfers between devices: none -> 16.4 us  [the longest x8 16.3 us: shards(): lax.ppermute(going_up, 'dev', [(d, (d + 1) % ways) for d in range(ways)])]
    ppermute x3, starting transfers between devices: 21.2 us -> 13.6 us  [with_halo(): before = lax.ppermute(last, axis, up)]
  transfers between devices with their start and end apart: 10 -> 25, of which waited for: 6 -> 14; matrix products, arithmetic and copies ran while one was open for 1% -> 1% of each run, Pallas kernels for 0% -> 0%
where the time goes in v1:
time: 519 us; the launch traced here: 509 us
  waiting for transfers between devices  345 us (66%)
  starting transfers between devices  51.5 us (10%)
  local copies, waits for them, and re-layouts  44 us (8%)
  matrix products  26.3 us (5%)
  other arithmetic  15.8 us (3%)
  between operations  14.5 us (3%)
  loops' own time  12.2 us (2%)
    unnamed x4, waiting for transfers between devices  319 us
    ppermute x7, starting transfers between devices, shards(): lax.ppermute(going_down, 'dev', [(d, (d - 1) % ways) for d in range(ways)])  31.4 us
    ppermute x8, waiting for transfers between devices, shards(): lax.ppermute(going_up, 'dev', [(d, (d + 1) % ways) for d in range(ways)])  16.3 us
    ppermute x3, starting transfers between devices, with_halo(): before = lax.ppermute(last, axis, up)  13.6 us
    another operation x7, loops' own time, when_true(): return lax.cond(flag, compute, skipped)  12.2 us
    another operation x13, local copies, waits for them, and re-layouts  11.9 us
  transfers between devices with their start and end apart: 25, of which 14 were waited for; matrix products, arithmetic and copies ran while one was open for 1% of the time, Pallas kernels for 0%

profile of v1, /device:TPU:0, one launch (start us, length us, event | category | flops | bytes accessed | tf_op | source)
XLA Modules:
  0.0 509.0 jit_solution(7866734774150191041)
XLA Ops:
  6.5 40.0 %conditional.8 = (bf16[5,1408]{1,0:T(8,128)(2,1)S(1)}, bf16[320,1408]{1,0:T(8,128)(2,1)}) conditional(s32[]{:T(128)} %convert_element_type.90, () %tuple.65, (bf16[5,64,1408]{2,1,0:T(8,128)(2,1)}, f32[1,1408]{1,0:T(1,128)}, bf16[1408,4224]{1,0:T(8,128)(2,1)}, bf16[1408,1408]{1,0:T(8,128)(2,1)}) %tuple.148), branch_computations={%region_0.0_spmd, %region_1.0_spmd} | conditional | flops 5198732288 | bytes 54580020 | solution.py:42
  10.3 9.1 %convolution_convert_fusion.1 = bf16[320,4224]{1,0:T(8,128)(2,1)S(1)} fusion(bf16[320,1408]{1,0:T(8,128)(2,1)S(1)} %fusion.44, bf16[1408,4224]{1,0:T(8,128)(2,1)} %get-tuple-element.100), kind=kOutput, calls=%fused_computation.55 | convolution fusion | flops 3807682560 | bytes 15499264 | tf_op jit(solution)/shard_map/cond/branch_1_fun/dot_general | solution.py:99
  19.4 8.5 %reshape.116 = bf16[5,64,3,16,88]{4,3,2,1,0:T(8,128)(2,1)} reshape(bf16[320,4224]{1,0:T(8,128)(2,1)S(1)} %convolution_convert_fusion.1) | data formatting | bytes 5406720 | tf_op jit(solution)/shard_map/cond/branch_1_fun/reshape | solution.py:100
  39.6 5.3 %convolution_add_fusion = f32[320,1408]{1,0:T(8,128)} fusion(bf16[320,1408]{1,0:T(8,128)(2,1)} %reshape.117, bf16[1408,1408]{1,0:T(8,128)(2,1)} %get-tuple-element.101, bf16[320,1408]{1,0:T(8,128)(2,1)S(1)} %bitcast.143), kind=kOutput, calls=%fused_computation.56 | convolution fusion | flops 1269678080 | bytes 7569408 | tf_op jit(solution)/shard_map/cond/branch_1_fun/dot_general | solution.py:115
  49.3 4.9 collective-permute-start.2
  55.7 4.4 collective-permute-start.4
  61.6 4.4 collective-permute-start.6
  67.5 4.4 collective-permute-start.8
  73.5 4.4 collective-permute-start.10
  79.4 4.4 collective-permute-start.12
  85.3 4.4 collective-permute-start.14
  91.2 5.9 %collective-permute-done.15 = bf16[5,1408]{1,0:T(8,128)(2,1)S(1)} collective-permute-done((bf16[5,1408]{1,0:T(8,128)(2,1)S(1)}, bf16[5,1408]{1,0:T(8,128)(2,1)S(1)}, u32[]{:S(2)}, u32[]{:S(2)}) %collective-permute-start.15) | collective-permute-done | bytes 14112 | tf_op jit(solution)/shard_map/ppermute | solution.py:128
  97.2 4.4 conditional.9
  118.7 6.1 %conditional.10 = (f32[3,16,128,384]{3,2,1,0:T(8,128)}, f32[3,16,128]{2,1,0:T(8,128)S(1)}, bf16[384,1408]{0,1:T(8,128)(2,1)}) conditional(s32[]{:T(128)} %convert_element_type.91, () %tuple.63, (pred[3,384]{1,0:T(4,128)(4,1)S(1)}, bf16[3,128,16,88]{1,0,3,2:T(4,128)(2,1)}, bf16[3,384,16,88]{1,3,2,0:T(8,128)(2,1)S(1)}, ...), branch_computations={%region_9.10_spmd, %region_10.13_spmd} | conditional | flops 856958976 | bytes 60534224 | solution.py:42
  118.7 4.8 broadcast.169
  124.8 6.0 %conditional.11 = (f32[3,16,128]{2,0,1:T(4,128)S(1)}, bf16[384,1408]{0,1:T(8,128)(2,1)}, bf16[384,1408]{0,1:T(8,128)(2,1)}) conditional(s32[]{:T(128)} %convert_element_type.91, () %tuple.72, (bf16[384,1408]{1,0:T(8,128)(2,1)}, bf16[1408,1408]{1,0:T(8,128)(2,1)}, bf16[384,1408]{0,1:T(8,128)(2,1)}, bf16[3,384,16,88]{1,3,2,0:T(8,128)(2,1)}, ...), branch_computations={%region_13.14_spmd, %region_14.16_spmd} | conditional | flops 2363320320 | bytes 39649360 | solution.py:42
  134.7 6.4 %collective-permute-start.18 = (bf16[128,2816]{0,1:T(8,128)(2,1)S(1)}, bf16[128,2816]{0,1:T(8,128)(2,1)S(1)}, u32[]{:S(2)}, u32[]{:S(2)}) collective-permute-start(bf16[128,2816]{0,1:T(8,128)(2,1)S(1)} %get-tuple-element.626), channel_id=1, source_target_pairs={{0,1},{1,2},{2,3},{3,4},{4,5},{5,6},{6,7},{7,8},{8,9},{9,10},{10,1... | collective-permute-start | bytes 2162696 | tf_op jit(solution)/shard_map/ppermute | solution.py:26
  142.4 5.0 collective-permute-start.20
  155.0 8.4 %conditional.13 = (f32[80,1408]{1,0:T(8,128)}) conditional(s32[]{:T(128)} %convert_element_type.91, () %tuple.71, (f32[384,1]{0,1:T(1,128)S(1)}, bf16[384,1408]{0,1:T(8,128)(2,1)}, bf16[384,2816]{0,1:T(8,128)(2,1)S(1)}, bf16[1408,4224]{1,0:T(8,128)(2,1)}, f32[1,1408]{1,0:T(1,128)}, /*index=5*/f32[384,1408]{1,0:T(8,128)}, ...), branch_computations={%region_18.19_spmd, %region_19.21_spmd} | conditional | flops 5097455616 | bytes 36246600 | solution.py:42
  164.8 215.3 %all-reduce.4.cloned.1.call-done = f32[80,1408]{1,0:T(8,128)} async-done(((f32[80,1408]{1,0:T(8,128)}), f32[80,1408]{1,0:T(8,128)}) %all-reduce.4.cloned.1.call-update) | async-done | bytes 450576
  382.2 4.7 collective-permute-done.22
  388.4 10.3 %conditional.15 = (f32[1408,1408]{1,0:T(8,128)}) conditional(s32[]{:T(128)} %convert_element_type.90, (bf16[384,1408]{0,1:T(8,128)(2,1)}, bf16[384,1408]{1,0:T(8,128)(2,1)S(1)}) %tuple.142, (bf16[320,1408]{1,0:T(8,128)(2,1)}, f32[320,1408]{1,0:T(8,128)S(1)}) %tuple.78), branch_computations={%region_24.25_spmd, %region_25.26_spmd} | conditional | flops 7612661760 | bytes 10633224 | solution.py:280
  388.4 10.3 %fusion.83 = f32[1408,1408]{1,0:T(8,128)} fusion(bf16[320,1408]{1,0:T(8,128)(2,1)} %get-tuple-element.136, f32[320,1408]{1,0:T(8,128)S(1)} %get-tuple-element.137), kind=kOutput, calls=%fused_computation.129 | convolution fusion | flops 7612661760 | bytes 10633216 | tf_op jit(solution)/shard_map/cond/branch_1_fun/dot_general | solution.py:52
  398.7 103.3 %reduce-scatter.4.cloned.1.call-done = f32[88,1408]{1,0:T(8,128)} async-done(((f32[1408,1408]{1,0:T(8,128)}), f32[88,1408]{1,0:T(8,128)}) %reduce-scatter.4.cloned.1.call-update) | async-done | bytes 495632
  (104 shorter events, 74.3 us)
Async XLA Ops:
  6.5 373.5 %all-reduce.4.cloned.1.call-start = ((), (), s32[]{:S(2)}) async-start(), calls=%async_computation.1 | async-start | bytes 901120
  49.3 6.4 %collective-permute-start.1 = (bf16[5,1408]{1,0:T(8,128)(2,1)S(1)}, bf16[5,1408]{1,0:T(8,128)(2,1)S(1)}, u32[]{:S(2)}, u32[]{:S(2)}) collective-permute-start(bf16[5,1408]{1,0:T(8,128)(2,1)S(1)} %collective-permute-done), channel_id=1, source_target_pairs={{0,1},{1,2},{2,3},{3,4},{4,5},{5,6},{6,7},{7,8},{8,9},{9,10},{10,1... | collective-permute-start | bytes 42248 | tf_op jit(solution)/shard_map/ppermute | solution.py:128
  49.3 6.4 %collective-permute-start.2 = (bf16[5,1408]{1,0:T(8,128)(2,1)S(1)}, bf16[5,1408]{1,0:T(8,128)(2,1)S(1)}, u32[]{:S(2)}, u32[]{:S(2)}) collective-permute-start(bf16[5,1408]{1,0:T(8,128)(2,1)S(1)} %collective-permute-done), channel_id=1, source_target_pairs={{0,15},{1,0},{2,1},{3,2},{4,3},{5,4},{6,5},{7,6},{8,7},{9,8},{10,9... | collective-permute-start | bytes 42248 | tf_op jit(solution)/shard_map/ppermute | solution.py:131
  55.7 5.9 %collective-permute-start.3 = (bf16[5,1408]{1,0:T(8,128)(2,1)S(1)}, bf16[5,1408]{1,0:T(8,128)(2,1)S(1)}, u32[]{:S(2)}, u32[]{:S(2)}) collective-permute-start(bf16[5,1408]{1,0:T(8,128)(2,1)S(1)} %collective-permute-done.1), channel_id=1, source_target_pairs={{0,1},{1,2},{2,3},{3,4},{4,5},{5,6},{6,7},{7,8},{8,9},{9,10},{10,1... | collective-permute-start | bytes 42248 | tf_op jit(solution)/shard_map/ppermute | solution.py:128
  55.7 5.9 %collective-permute-start.4 = (bf16[5,1408]{1,0:T(8,128)(2,1)S(1)}, bf16[5,1408]{1,0:T(8,128)(2,1)S(1)}, u32[]{:S(2)}, u32[]{:S(2)}) collective-permute-start(bf16[5,1408]{1,0:T(8,128)(2,1)S(1)} %collective-permute-done.2), channel_id=1, source_target_pairs={{0,15},{1,0},{2,1},{3,2},{4,3},{5,4},{6,5},{7,6},{8,7},{9,8},{10,9... | collective-permute-start | bytes 42248 | tf_op jit(solution)/shard_map/ppermute | solution.py:131
  61.6 5.9 %collective-permute-start.5 = (bf16[5,1408]{1,0:T(8,128)(2,1)S(1)}, bf16[5,1408]{1,0:T(8,128)(2,1)S(1)}, u32[]{:S(2)}, u32[]{:S(2)}) collective-permute-start(bf16[5,1408]{1,0:T(8,128)(2,1)S(1)} %collective-permute-done.3), channel_id=1, source_target_pairs={{0,1},{1,2},{2,3},{3,4},{4,5},{5,6},{6,7},{7,8},{8,9},{9,10},{10,1... | collective-permute-start | bytes 42248 | tf_op jit(solution)/shard_map/ppermute | solution.py:128
  61.6 5.9 %collective-permute-start.6 = (bf16[5,1408]{1,0:T(8,128)(2,1)S(1)}, bf16[5,1408]{1,0:T(8,128)(2,1)S(1)}, u32[]{:S(2)}, u32[]{:S(2)}) collective-permute-start(bf16[5,1408]{1,0:T(8,128)(2,1)S(1)} %collective-permute-done.4), channel_id=1, source_target_pairs={{0,15},{1,0},{2,1},{3,2},{4,3},{5,4},{6,5},{7,6},{8,7},{9,8},{10,9... | collective-permute-start | bytes 42248 | tf_op jit(solution)/shard_map/ppermute | solution.py:131
  67.5 5.9 %collective-permute-start.7 = (bf16[5,1408]{1,0:T(8,128)(2,1)S(1)}, bf16[5,1408]{1,0:T(8,128)(2,1)S(1)}, u32[]{:S(2)}, u32[]{:S(2)}) collective-permute-start(bf16[5,1408]{1,0:T(8,128)(2,1)S(1)} %collective-permute-done.5), channel_id=1, source_target_pairs={{0,1},{1,2},{2,3},{3,4},{4,5},{5,6},{6,7},{7,8},{8,9},{9,10},{10,1... | collective-permute-start | bytes 42248 | tf_op jit(solution)/shard_map/ppermute | solution.py:128
  67.5 5.9 %collective-permute-start.8 = (bf16[5,1408]{1,0:T(8,128)(2,1)S(1)}, bf16[5,1408]{1,0:T(8,128)(2,1)S(1)}, u32[]{:S(2)}, u32[]{:S(2)}) collective-permute-start(bf16[5,1408]{1,0:T(8,128)(2,1)S(1)} %collective-permute-done.6), channel_id=1, source_target_pairs={{0,15},{1,0},{2,1},{3,2},{4,3},{5,4},{6,5},{7,6},{8,7},{9,8},{10,9... | collective-permute-start | bytes 42248 | tf_op jit(solution)/shard_map/ppermute | solution.py:131
  73.4 5.9 %collective-permute-start.9 = (bf16[5,1408]{1,0:T(8,128)(2,1)S(1)}, bf16[5,1408]{1,0:T(8,128)(2,1)S(1)}, u32[]{:S(2)}, u32[]{:S(2)}) collective-permute-start(bf16[5,1408]{1,0:T(8,128)(2,1)S(1)} %collective-permute-done.7), channel_id=1, source_target_pairs={{0,1},{1,2},{2,3},{3,4},{4,5},{5,6},{6,7},{7,8},{8,9},{9,10},{10,1... | collective-permute-start | bytes 42248 | tf_op jit(solution)/shard_map/ppermute | solution.py:128
  73.5 5.9 %collective-permute-start.10 = (bf16[5,1408]{1,0:T(8,128)(2,1)S(1)}, bf16[5,1408]{1,0:T(8,128)(2,1)S(1)}, u32[]{:S(2)}, u32[]{:S(2)}) collective-permute-start(bf16[5,1408]{1,0:T(8,128)(2,1)S(1)} %collective-permute-done.8), channel_id=1, source_target_pairs={{0,15},{1,0},{2,1},{3,2},{4,3},{5,4},{6,5},{7,6},{8,7},{9,8},{10,9... | collective-permute-start | bytes 42248 | tf_op jit(solution)/shard_map/ppermute | solution.py:131
  79.4 5.9 %collective-permute-start.11 = (bf16[5,1408]{1,0:T(8,128)(2,1)S(1)}, bf16[5,1408]{1,0:T(8,128)(2,1)S(1)}, u32[]{:S(2)}, u32[]{:S(2)}) collective-permute-start(bf16[5,1408]{1,0:T(8,128)(2,1)S(1)} %collective-permute-done.9), channel_id=1, source_target_pairs={{0,1},{1,2},{2,3},{3,4},{4,5},{5,6},{6,7},{7,8},{8,9},{9,10},{10,1... | collective-permute-start | bytes 42248 | tf_op jit(solution)/shard_map/ppermute | solution.py:128
  79.4 5.9 %collective-permute-start.12 = (bf16[5,1408]{1,0:T(8,128)(2,1)S(1)}, bf16[5,1408]{1,0:T(8,128)(2,1)S(1)}, u32[]{:S(2)}, u32[]{:S(2)}) collective-permute-start(bf16[5,1408]{1,0:T(8,128)(2,1)S(1)} %collective-permute-done.10), channel_id=1, source_target_pairs={{0,15},{1,0},{2,1},{3,2},{4,3},{5,4},{6,5},{7,6},{8,7},{9,8},{10,9... | collective-permute-start | bytes 42248 | tf_op jit(solution)/shard_map/ppermute | solution.py:131
  85.3 5.9 %collective-permute-start.13 = (bf16[5,1408]{1,0:T(8,128)(2,1)S(1)}, bf16[5,1408]{1,0:T(8,128)(2,1)S(1)}, u32[]{:S(2)}, u32[]{:S(2)}) collective-permute-start(bf16[5,1408]{1,0:T(8,128)(2,1)S(1)} %collective-permute-done.11), channel_id=1, source_target_pairs={{0,1},{1,2},{2,3},{3,4},{4,5},{5,6},{6,7},{7,8},{8,9},{9,10},{10,1... | collective-permute-start | bytes 42248 | tf_op jit(solution)/shard_map/ppermute | solution.py:128
  85.3 5.9 %collective-permute-start.14 = (bf16[5,1408]{1,0:T(8,128)(2,1)S(1)}, bf16[5,1408]{1,0:T(8,128)(2,1)S(1)}, u32[]{:S(2)}, u32[]{:S(2)}) collective-permute-start(bf16[5,1408]{1,0:T(8,128)(2,1)S(1)} %collective-permute-done.12), channel_id=1, source_target_pairs={{0,15},{1,0},{2,1},{3,2},{4,3},{5,4},{6,5},{7,6},{8,7},{9,8},{10,9... | collective-permute-start | bytes 42248 | tf_op jit(solution)/shard_map/ppermute | solution.py:131
  91.2 5.9 %collective-permute-start.15 = (bf16[5,1408]{1,0:T(8,128)(2,1)S(1)}, bf16[5,1408]{1,0:T(8,128)(2,1)S(1)}, u32[]{:S(2)}, u32[]{:S(2)}) collective-permute-start(bf16[5,1408]{1,0:T(8,128)(2,1)S(1)} %collective-permute-done.13), channel_id=1, source_target_pairs={{0,1},{1,2},{2,3},{3,4},{4,5},{5,6},{6,7},{7,8},{8,9},{9,10},{10,1... | collective-permute-start | bytes 42248 | tf_op jit(solution)/shard_map/ppermute | solution.py:128
  106.8 5.9 %collective-permute-start.16 = (bf16[128,2816]{0,1:T(8,128)(2,1)}, bf16[128,2816]{0,1:T(8,128)(2,1)}, u32[]{:S(2)}, u32[]{:S(2)}) collective-permute-start(bf16[128,2816]{0,1:T(8,128)(2,1)} %get-tuple-element.630), channel_id=1, source_target_pairs={{0,1},{1,2},{2,3},{3,4},{4,5},{5,6},{6,7},{7,8},{8,9},{9,10},{10,1... | collective-permute-start | bytes 2162696 | tf_op jit(solution)/shard_map/ppermute | solution.py:26
  109.0 4.2 collective-permute-start.17
  134.7 17.1 %collective-permute-start.18 = (bf16[128,2816]{0,1:T(8,128)(2,1)S(1)}, bf16[128,2816]{0,1:T(8,128)(2,1)S(1)}, u32[]{:S(2)}, u32[]{:S(2)}) collective-permute-start(bf16[128,2816]{0,1:T(8,128)(2,1)S(1)} %get-tuple-element.626), channel_id=1, source_target_pairs={{0,1},{1,2},{2,3},{3,4},{4,5},{5,6},{6,7},{7,8},{8,9},{9,10},{10,1... | collective-permute-start | bytes 2162696 | tf_op jit(solution)/shard_map/ppermute | solution.py:26
  141.1 10.7 %collective-permute-start.19 = (bf16[128,2816]{0,1:T(8,128)(2,1)S(1)}, bf16[128,2816]{0,1:T(8,128)(2,1)S(1)}, u32[]{:S(2)}, u32[]{:S(2)}) collective-permute-start(bf16[128,2816]{0,1:T(8,128)(2,1)S(1)} %get-tuple-element.627), channel_id=1, source_target_pairs={{1,0},{2,1},{3,2},{4,3},{5,4},{6,5},{7,6},{8,7},{9,8},{10,9},{11,1... | collective-permute-start | bytes 2162696 | tf_op jit(solution)/shard_map/ppermute | solution.py:27
  142.4 6.3 %collective-permute-start.20 = (f32[128,32]{0,1:T(8,128)S(1)}, f32[128,32]{0,1:T(8,128)S(1)}, u32[]{:S(2)}, u32[]{:S(2)}) collective-permute-start(f32[128,32]{0,1:T(8,128)S(1)} %get-tuple-element.632), channel_id=1, source_target_pairs={{0,1},{1,2},{2,3},{3,4},{4,5},{5,6},{6,7},{7,8},{8,9},{9,10},{10,1... | collective-permute-start | bytes 49160 | tf_op jit(solution)/shard_map/ppermute | solution.py:26
  147.4 4.3 collective-permute-start.21
  163.5 338.5 %reduce-scatter.4.cloned.1.call-start = ((), (), s32[]{:S(2)}) async-start(), calls=%async_computation.2 | async-start | bytes 8425472
  380.9 6.0 %collective-permute-start.22 = (f32[5,1408]{1,0:T(8,128)S(1)}, f32[5,1408]{1,0:T(8,128)S(1)}, u32[]{:S(2)}, u32[]{:S(2)}) collective-permute-start(f32[5,1408]{1,0:T(8,128)S(1)} %constant_dynamic-slice_fusion), channel_id=1, source_target_pairs={{16,0},{17,1},{18,2},{19,3},{20,4},{21,5},{22,6},{23,7},{24,8},{25... | collective-permute-start | bytes 84488 | tf_op jit(solution)/shard_map/ppermute | solution.py:16
  (10 other events, 221.5 us)
Sparse Core Ops, SparseCore 0:
  163.6 216.4 all-reduce.3
  398.8 103.0 reduce-scatter.3
